TPU v7x, 256 devices: a whole 4x4x8 slice. The times are simulated.
256 devices in a mesh: inp: 128 (over x, y, z), tm: 2 (over core).
Axes of the slice: x: 4, y: 4, z: 8, core: 2. Of those that a mesh axis runs over, the one named last changes fastest.
Arguments:
- samples: bfloat16 [512, 2, 131, 2048], P('inp', 'tm'), may hold values from -6 to 6
- pfb_weights: float32 [4, 2048], replicated, may hold values from -3 to 3
Outputs:
- visibility: float32 [1024, 512, 512], P(('inp', 'tm'))
All inputs are finite; a program needn't handle non-finite values.
Results may differ from a plain program's by a relative error of at most 0.0046.
Values may be sent and summed in bfloat16 or wider, within the bound.
A program may use at most 128 MiB of HBM per device.

v0:
```python
import math

import jax
import jax.numpy as jnp
from jax import lax
from jax.sharding import PartitionSpec as P


def dft_table(channels, length):
    index_n = jnp.arange(length, dtype=jnp.int32)
    index_k = jnp.arange(channels, dtype=jnp.int32)
    phase = index_k[:, None] * index_n[None, :] % length
    angle = phase.astype(jnp.float32) * (2.0 * math.pi / length)
    return jnp.stack([jnp.cos(angle), -jnp.sin(angle)]).astype(jnp.bfloat16)


def correlate(turned):
    count, parts, inputs, spectra = turned.shape
    stacked = turned.reshape(count, parts * inputs, spectra)
    gram = jnp.einsum("cas,cbs->cab", stacked, stacked, preferred_element_type=jnp.float32)
    real_part = gram[:, :inputs, :inputs] + gram[:, inputs:, inputs:]
    imag_part = gram[:, inputs:, :inputs] - gram[:, :inputs, inputs:]
    rows = jnp.arange(inputs, dtype=jnp.int32)
    lower = rows[:, None] >= rows[None, :]
    return jnp.where(lower[None], real_part, imag_part)


def body(samples, pfb_weights):
    frames = samples[:, 0]
    taps = pfb_weights.shape[0]
    length = frames.shape[2]
    per_block = frames.shape[1] - taps + 1
    total = jnp.zeros((frames.shape[0], per_block, length), jnp.float32)
    for tap in range(taps):
        total = total + pfb_weights[tap] * frames[:, tap : tap + per_block].astype(jnp.float32)
    filtered = total.astype(jnp.bfloat16)
    table = dft_table(length // 2, length)
    spectra = jnp.einsum("rkn,asn->kras", table, filtered, preferred_element_type=jnp.float32)
    spectra = (spectra * math.sqrt(2.0 / length)).astype(jnp.bfloat16)
    count_all = per_block * lax.axis_size("tm")
    turned = lax.all_to_all(spectra, "inp", split_axis=0, concat_axis=2, tiled=True)
    partial_vis = correlate(turned)
    summed = lax.psum_scatter(partial_vis, "tm", scatter_dimension=0, tiled=True)
    return summed / count_all


def solution(mesh):
    placed = (P("inp", "tm", None, None), P())
    return jax.shard_map(
        body, mesh=mesh, in_specs=placed, out_specs=P(("inp", "tm"), None, None), check_vma=False
    )
```

profile of v0, /device:TPU:1, one launch (start us, length us, event | category | flops | bytes accessed | tf_op | source)
XLA Modules:
  0.0 180.2 jit_solution(5119319349028650657)
XLA Ops:
  6.5 0.0 copy-start.1
  6.5 0.0 copy-start
  6.5 33.6 %negate_convert_fusion = (bf16[1,1024,2048]{2,1,0:T(8,128)(2,1)S(1)}, bf16[1,1024,2048]{2,1,0:T(8,128)(2,1)S(1)}) fusion(), kind=kLoop, calls=%fused_computation.13 | loop fusion | flops 35651584 | bytes 8388608 | tf_op jit(solution)/shard_map/convert.1
  40.2 0.0 copy-done.1
  40.2 0.0 copy-done
  40.2 1.2 copy.19
  41.4 5.5 %fusion.20 = bf16[1024,2,4,128]{0,3,1,2:T(8,128)(2,1)S(1)} fusion(bf16[1,1024,2048]{2,1,0:T(8,128)(2,1)S(1)} %get-tuple-element.9, bf16[1,1024,2048]{2,1,0:T(8,128)(2,1)S(1)} %get-tuple-element.10, bf16[4,131,2048]{2,1,0:T(8,128)(2,1)S(1)} %bitcast.33, f32[2048]{0:T(1024)S(1)} %bitcast.36, f32[2048]{0:T(1024)S(1)} %bitcast.37, f32[2048]{0:T(1024)S(1)} %bitcast.35, ...), kind=kOutput, calls=%fused_computation.32 | convolution fusion | flops 4326424576 | bytes 18907136 | tf_op jit(solution)/shard_map/rkn,asn->kras/dot_general | solution.py:38
  47.0 4.0 %copy.13 = bf16[1024,2,4,128]{3,1,2,0:T(2,128)(2,1)} copy(bf16[1024,2,4,128]{0,3,1,2:T(8,128)(2,1)S(1)} %fusion.20) | data formatting | bytes 4194304 | tf_op jit(solution)/shard_map/convert_element_type | solution.py:39
  51.0 16.3 %all-to-all-start = ((bf16[1024,2,4,128]{3,1,2,0:T(2,128)(2,1)}), bf16[1024,2,4,128]{3,1,2,0:T(2,128)(2,1)S(1)}, u32[]{:S(2)}, u32[]{:S(2)}) async-start(bf16[1024,2,4,128]{3,1,2,0:T(2,128)(2,1)} %copy.13), calls=%async_computation | async-start | bytes 4194304 | tf_op jit(solution)/shard_map/all_to_all | solution.py:41
  67.3 0.2 reduce-scatter.2.cloned.1.call-start
  67.6 0.1 iota_compare_fusion
  67.7 52.4 %all-to-all-done = bf16[1024,2,4,128]{3,1,2,0:T(2,128)(2,1)S(1)} async-done(((bf16[1024,2,4,128]{3,1,2,0:T(2,128)(2,1)}), bf16[1024,2,4,128]{3,1,2,0:T(2,128)(2,1)S(1)}, u32[]{:S(2)}, u32[]{:S(2)}) %all-to-all-start) | async-done | bytes 2097184 | tf_op jit(solution)/shard_map/all_to_all | solution.py:41
  120.1 0.3 copy.20
  120.3 1.6 copy.15
  122.0 13.1 %fusion.25 = f32[8,1024,1024]{2,1,0:T(8,128)} fusion(bf16[8,1024,128]{2,1,0:T(8,128)(2,1)S(1)} %bitcast.31), kind=kOutput, calls=%fused_computation.36 | convolution fusion | flops 2147483648 | bytes 35651584 | tf_op jit(solution)/shard_map/cas,cbs->cab/dot_general | solution.py:20
  135.1 16.3 %fusion.3 = f32[8,512,512]{2,1,0:T(8,128)} fusion(f32[8,1024,1024]{2,1,0:T(8,128)} %fusion.25, pred[512,512]{1,0:T(8,128)(4,1)S(1)} %iota_compare_fusion), kind=kLoop, calls=%fused_computation.7 | loop fusion | flops 6291456 | bytes 42205184 | tf_op jit(solution)/shard_map/jit(_where)/select_n | solution.py:25
  151.4 0.0 reduce-scatter.2.cloned.1.call-update
  151.4 17.2 %reduce-scatter.2.cloned.1.call-done = f32[4,512,512]{2,1,0:T(8,128)} async-done(((f32[8,512,512]{2,1,0:T(8,128)}), f32[4,512,512]{2,1,0:T(8,128)}) %reduce-scatter.2.cloned.1.call-update) | async-done | bytes 4194320 | tf_op jit(solution)/shard_map/reduce_scatter | solution.py:43
  168.6 4.7 %broadcast_multiply_fusion = f32[4,512,512]{2,1,0:T(8,128)} fusion(f32[4,512,512]{2,1,0:T(8,128)} %reduce-scatter.2.cloned.1.call-done), kind=kLoop, calls=%fused_computation.27 | loop fusion | flops 1048576 | bytes 8388608 | tf_op jit(solution)/shard_map/div | solution.py:44
  (1 shorter events, 0.0 us)
Async XLA Ops:
  6.5 33.6 %copy-start.1 = (f32[4,2048]{1,0:T(4,128)S(1)}, f32[4,2048]{1,0:T(4,128)}, u32[]{:S(2)}) copy-start(f32[4,2048]{1,0:T(4,128)} %param.3) | copy-start | bytes 98308
  6.5 33.7 %copy-start = (bf16[4,1,131,2048]{3,0,2,1:T(4,128)(2,1)S(1)}, bf16[4,1,131,2048]{3,0,2,1:T(4,128)(2,1)}, u32[]{:S(2)}) copy-start(bf16[4,1,131,2048]{3,0,2,1:T(4,128)(2,1)} %param.2) | copy-start | bytes 6438916
  51.0 69.0 %all-to-all-start = ((bf16[1024,2,4,128]{3,1,2,0:T(2,128)(2,1)}), bf16[1024,2,4,128]{3,1,2,0:T(2,128)(2,1)S(1)}, u32[]{:S(2)}, u32[]{:S(2)}) async-start(bf16[1024,2,4,128]{3,1,2,0:T(2,128)(2,1)} %copy.13), calls=%async_computation | async-start | bytes 4194304 | tf_op jit(solution)/shard_map/all_to_all | solution.py:41
  67.3 101.3 %reduce-scatter.2.cloned.1.call-start = ((), (), s32[]{:S(2)}) async-start(), calls=%async_computation.2 | async-start | bytes 12582912 | tf_op jit(solution)/shard_map/reduce_scatter | solution.py:43
Sparse Core Ops, SparseCore 0:
  151.6 17.0 reduce-scatter.1
where the time goes:
time: 180 us
  waiting for transfers between devices  69.6 us (39%)
  other arithmetic  54.8 us (30%)
  matrix products  18.7 us (10%)
  starting transfers between devices  16.6 us (9%)
  between operations  13.5 us (8%)
  local copies, waits for them, and re-layouts  7.16 us (4%)
    all_to_all x1, waiting for transfers between devices, body(): lax.all_to_all(spectra, 'inp', split_axis=0, concat_axis=2, tiled=True)  52.4 us
    another operation x1, other arithmetic  33.6 us
    reduce_scatter x1, waiting for transfers between devices, body(): lax.psum_scatter(partial_vis, 'tm', scatter_dimension=0, tiled=True)  17.2 us
    select_n x1, other arithmetic, correlate(): return jnp.where(lower[None], real_part, imag_part)  16.3 us
    all_to_all x1, starting transfers between devices, body(): lax.all_to_all(spectra, 'inp', split_axis=0, concat_axis=2, tiled=True)  16.3 us
    dot_general x1, matrix products, correlate(): jnp.einsum('cas,cbs->cab', stacked, stacked, preferred_element_type=jnp.f...  13.1 us
    dot_general x1, matrix products, body(): jnp.einsum('rkn,asn->kras', table, filtered, preferred_element_type=jnp.f...  5.55 us
    div x1, other arithmetic, body(): return summed / count_all  4.73 us
  transfers between devices with their start and end apart: 2, of which 2 were waited for; matrix products, arithmetic and copies ran while one was open for 0% of the time, Pallas kernels for 0%

commit v1 on v0

v1 whole, which is shorter than its diff:
```python
import functools
import math

import jax
import jax.numpy as jnp
import ml_dtypes
import numpy as np
from jax import lax
from jax.experimental import pallas as pl
from jax.experimental.pallas import tpu as pltpu
from jax.sharding import PartitionSpec as P

MESH = pl.DeviceIdType.MESH
VMEM_LIMIT = 48 * 1024 * 1024
LAYERS = 8
CORES = 2


def dft_table(channels, length, scale):
    phase = np.arange(channels)[:, None] * np.arange(length)[None, :] % length
    angle = np.arange(length) * (2.0 * math.pi / length)
    rows = np.stack([np.cos(angle)[phase], -np.sin(angle)[phase]], axis=1) * scale
    return rows.reshape(channels * 2, length).astype(ml_dtypes.bfloat16)


def turn_kernel(
    samples, weights, table, turned, frames, filtered, coeffs, outbox, inbox, table_sem, send_sem, recv_sem
):
    position, core = lax.axis_index("inp"), lax.axis_index("tm")
    group, layer = position // LAYERS, position % LAYERS
    me = position * CORES + core
    groups, rows, length = coeffs.shape
    devices = groups * LAYERS * CORES
    inputs, _, _ = samples.shape
    spectra = filtered.shape[0] // inputs
    taps = weights.shape[0]
    peers = LAYERS * CORES

    def fetch(step):
        chunk = lax.rem(group + step, groups)
        return pltpu.make_async_copy(table.at[chunk], coeffs.at[step], table_sem.at[step])

    def start_fetch(step, carry):
        fetch(step).start()
        return carry

    lax.fori_loop(0, groups, start_fetch, 0)

    barrier = pltpu.get_barrier_semaphore()

    def greet(step, carry):
        other = lax.rem(me + step, devices)
        pl.semaphore_signal(
            barrier, inc=1, device_id=(other // CORES, lax.rem(other, CORES)), device_id_type=MESH
        )
        return carry

    lax.fori_loop(1, devices, greet, 0)

    for a in range(inputs):
        def columns(j, carry):
            cols = pl.ds(pl.multiple_of(j * 128, 128), 128)
            frames[...] = samples[a, :, cols].astype(jnp.float32)
            total = weights[0:1, cols] * frames[0:spectra]
            for tap in range(1, taps):
                total = total + weights[tap : tap + 1, cols] * frames[tap : tap + spectra]
            filtered[a * spectra : (a + 1) * spectra, cols] = total.astype(jnp.bfloat16)
            return carry

        lax.fori_loop(0, length // 128, columns, 0)

    pl.semaphore_wait(barrier, devices - 1)

    half = filtered.shape[0] // 2

    def send_group(step, carry):
        fetch(step).wait()
        found = lax.dot_general(
            coeffs[step], filtered[...], (((1,), (1,)), ((), ())), preferred_element_type=jnp.float32
        )
        found = found.reshape(peers, rows // peers, 2 * half)
        message = jnp.concatenate([found[:, :, :half], found[:, :, half:]], axis=1)
        outbox[pl.ds(step * peers, peers)] = message.astype(jnp.bfloat16)
        to_group = lax.rem(group + step, groups)
        for turn in (4, 3, 5, 2, 6, 1, 7, 0):
            for flip in (0, 1):
                to_layer = lax.rem(layer + turn, LAYERS)
                to_core = lax.rem(core + flip, CORES)
                source = outbox.at[step * peers + to_layer * CORES + to_core]

                def remote():
                    pltpu.make_async_remote_copy(
                        src_ref=source,
                        dst_ref=inbox.at[core, position],
                        send_sem=send_sem,
                        recv_sem=recv_sem.at[group],
                        device_id=(to_group * LAYERS + to_layer, to_core),
                        device_id_type=MESH,
                    ).start()

                if turn == 0 and flip == 0:
                    pl.when(step > 0)(remote)

                    @pl.when(step == 0)
                    def _():
                        pltpu.make_async_copy(source, inbox.at[core, position], recv_sem.at[group]).start()
                else:
                    remote()
        return carry

    lax.fori_loop(0, groups, send_group, 0)

    size = rows * 2
    out_row = lax.broadcasted_iota(jnp.int32, (size, size), 0)
    in_row = lax.broadcasted_iota(jnp.int32, (size, size), 1)
    wanted = (
        (out_row % 2) * (size // 2)
        + (out_row // 4 % LAYERS) * 16
        + (out_row // 2 % 2) * 8
        + (out_row // 64) * 2
        + (out_row // 32 % 2)
    )
    permute = jnp.where(in_row == wanted, 1.0, 0.0).astype(jnp.bfloat16)

    def receive_group(step, carry):
        from_group = lax.rem(group + groups - step, groups)
        landed = inbox.at[:, pl.ds(from_group * LAYERS, LAYERS)]
        pltpu.make_async_copy(landed, landed, recv_sem.at[from_group]).wait()
        first = inbox[0, pl.ds(from_group * LAYERS, LAYERS)].reshape(rows, half)
        second = inbox[1, pl.ds(from_group * LAYERS, LAYERS)].reshape(rows, half)
        top = jnp.concatenate([first[:, : half // 2], second[:, : half // 2]], axis=1)
        bottom = jnp.concatenate([first[:, half // 2 :], second[:, half // 2 :]], axis=1)
        ordered = jnp.dot(
            permute, jnp.concatenate([top, bottom], axis=0), preferred_element_type=jnp.float32
        ).astype(jnp.bfloat16)
        place = pl.ds(pl.multiple_of(from_group * 32, 32), 32)
        for plane in range(8):
            turned[plane, place, :] = ordered[plane * 32 : plane * 32 + 32]
        return carry

    lax.fori_loop(0, groups, receive_group, 0)
    sent = outbox.at[pl.ds(0, devices - 1)]
    pltpu.make_async_copy(sent, sent, send_sem).wait()


def gram_kernel(planes, out):
    real, imag = planes[0], planes[1]
    size = out.shape[1]
    half = size // 2

    def times(a, b):
        return lax.dot_general(a, b, (((1,), (1,)), ((), ())), preferred_element_type=jnp.float32)

    for i in range(2):
        for j in range(2):
            ri, rj = real[i * half : (i + 1) * half], real[j * half : (j + 1) * half]
            mi, mj = imag[i * half : (i + 1) * half], imag[j * half : (j + 1) * half]
            place = (0, slice(i * half, (i + 1) * half), slice(j * half, (j + 1) * half))
            if i > j:
                out[place] = times(ri, rj) + times(mi, mj)
            elif i < j:
                out[place] = times(mi, rj) - times(ri, mj)
            else:
                row = lax.broadcasted_iota(jnp.int32, (half, half), 0)
                column = lax.broadcasted_iota(jnp.int32, (half, half), 1)
                same = times(ri, rj) + times(mi, mj)
                cross = times(mi, rj) - times(ri, mj)
                out[place] = jnp.where(row >= column, same, cross)


def body(samples, pfb_weights):
    frames = samples[:, 0]
    inputs, count, length = frames.shape
    taps = pfb_weights.shape[0]
    spectra = count - taps + 1
    channels = length // 2
    positions = lax.axis_size("inp")
    groups = positions // LAYERS
    devices = positions * CORES
    rows = 2 * channels // groups
    all_spectra = spectra * CORES
    scale = math.sqrt(2.0 / length) / math.sqrt(all_spectra)
    table = jnp.asarray(dft_table(channels, length, scale).reshape(groups, rows, length))
    per_device = channels // devices
    width = inputs * spectra // 2
    deep = 2 * per_device * 2
    turned = pl.pallas_call(
        turn_kernel,
        out_shape=jax.ShapeDtypeStruct((per_device * 2, inputs * positions, all_spectra), jnp.bfloat16),
        in_specs=[
            pl.BlockSpec(memory_space=pltpu.VMEM),
            pl.BlockSpec(memory_space=pltpu.VMEM),
            pl.BlockSpec(memory_space=pl.ANY),
        ],
        out_specs=pl.BlockSpec(memory_space=pltpu.VMEM),
        scratch_shapes=[
            pltpu.VMEM((count, 128), jnp.float32),
            pltpu.VMEM((inputs * spectra, length), jnp.bfloat16),
            pltpu.VMEM((groups, rows, length), jnp.bfloat16),
            pltpu.VMEM((devices, deep, width), jnp.bfloat16),
            pltpu.VMEM((CORES, positions, deep, width), jnp.bfloat16),
            pltpu.SemaphoreType.DMA((groups,)),
            pltpu.SemaphoreType.DMA,
            pltpu.SemaphoreType.DMA((groups,)),
        ],
        compiler_params=pltpu.CompilerParams(
            collective_id=0, has_side_effects=True, vmem_limit_bytes=VMEM_LIMIT
        ),
    )(frames, pfb_weights, table)
    total = inputs * positions
    return pl.pallas_call(
        gram_kernel,
        grid=(per_device,),
        out_shape=jax.ShapeDtypeStruct((per_device, total, total), jnp.float32),
        in_specs=[pl.BlockSpec((2, total, all_spectra), lambda c: (c, 0, 0))],
        out_specs=pl.BlockSpec((1, total, total), lambda c: (c, 0, 0)),
        compiler_params=pltpu.CompilerParams(vmem_limit_bytes=VMEM_LIMIT),
    )(turned)


def solution(mesh):
    placed = (P("inp", "tm", None, None), P())
    return jax.shard_map(
        body, mesh=mesh, in_specs=placed, out_specs=P(("inp", "tm"), None, None), check_vma=False
    )
```

time: 180 us -> 71.4 us (0.40)
  waiting for transfers between devices: 69.6 us -> 0 us
  Pallas kernels: 0 us -> 68.5 us
  other arithmetic: 54.8 us -> 0 us
  matrix products: 18.7 us -> 0 us
  starting transfers between devices: 16.6 us -> 0 us
  between operations: 13.5 us -> 0.02 us
  local copies, waits for them, and re-layouts: 7.16 us -> 2.79 us
    pallas_call x0 -> x2, Pallas kernels: none -> 68.5 us  [the longest x1 64.7 us: body(): pl.pallas_call(turn_kernel, out_shape=jax.ShapeDtypeStruct((per_device *...]
    all_to_all x1 -> x0, waiting for transfers between devices: 52.4 us -> none  [body(): lax.all_to_all(spectra, 'inp', split_axis=0, concat_axis=2, tiled=True)]
    another operation x1 -> x0, other arithmetic: 33.6 us -> none
    dot_general x2 -> x0, matrix products: 18.7 us -> none  [the longest x1 13.1 us: correlate(): jnp.einsum('cas,cbs->cab', stacked, stacked, preferred_element_type=jnp.f...]
    reduce_scatter x1 -> x0, waiting for transfers between devices: 17.2 us -> none  [body(): lax.psum_scatter(partial_vis, 'tm', scatter_dimension=0, tiled=True)]
    select_n x1 -> x0, other arithmetic: 16.3 us -> none  [correlate(): return jnp.where(lower[None], real_part, imag_part)]
    all_to_all x1 -> x0, starting transfers between devices: 16.3 us -> none  [body(): lax.all_to_all(spectra, 'inp', split_axis=0, concat_axis=2, tiled=True)]
    div x1 -> x0, other arithmetic: 4.73 us -> none  [body(): return summed / count_all]
  transfers between devices with their start and end apart: 2 -> 0, of which waited for: 2 -> 0; matrix products, arithmetic and copies ran while one was open for 0% -> 0% of each run, Pallas kernels for 0% -> 0%
where the time goes in v1:
time: 71.4 us; the launch traced here: 71.3 us
  Pallas kernels  68.5 us (96%)
  local copies, waits for them, and re-layouts  2.79 us (4%)
    pallas_call x1, Pallas kernels, body(): pl.pallas_call(turn_kernel, out_shape=jax.ShapeDtypeStruct((per_device *...  64.7 us
    pallas_call x1, Pallas kernels, body(): pl.pallas_call(gram_kernel, grid=(per_device,), out_shape=jax.ShapeDtypeS...  3.8 us
    unnamed x3, local copies, waits for them, and re-layouts  2.79 us

profile of v1, /device:TPU:1, one launch (start us, length us, event | category | flops | bytes accessed | tf_op | source)
XLA Modules:
  0.0 71.3 jit_solution(11619733406297537741)
XLA Ops:
  0.0 0.0 copy-start
  0.0 2.8 %copy.6 = bf16[4,1,131,2048]{3,2,0,1:T(8,128)(2,1)S(1)} copy(bf16[4,1,131,2048]{3,0,2,1:T(4,128)(2,1)} %param.3) | data formatting | bytes 4292608 | tf_op args[0]
  2.8 0.0 copy-done
  2.8 64.7 %shard_map.37.planes = bf16[8,512,256]{2,1,0:T(8,128)(2,1)S(1)} custom-call(bf16[4,131,2048]{2,1,0:T(8,128)(2,1)S(1)} %bitcast.3, f32[4,2048]{1,0:T(4,128)S(1)} %copy-done, bf16[16,128,2048]{2,1,0:T(8,128)(2,1)} %constant.2.clone.table), custom_call_target="tpu_custom_call" | custom-call | tf_op jit(solution)/shard_map/pallas_call | solution.py:187
  67.5 3.8 %shard_map.38 = f32[4,512,512]{2,1,0:T(8,128)} custom-call(bf16[8,512,256]{2,1,0:T(8,128)(2,1)S(1)} %shard_map.37.planes), custom_call_target="tpu_custom_call" | custom-call | tf_op jit(solution)/shard_map/pallas_call | solution.py:211
Async XLA Ops:
  0.0 2.8 %copy-start = (f32[4,2048]{1,0:T(4,128)S(1)}, f32[4,2048]{1,0:T(4,128)}, u32[]{:S(2)}) copy-start(f32[4,2048]{1,0:T(4,128)} %weights.1) | copy-start | bytes 98308

commit v2 on v1

--- a/solution.py
+++ b/solution.py
@@ -1,6 +1,5 @@
 import functools
 import math
-
 import jax
 import jax.numpy as jnp
 import ml_dtypes
@@ -24,14 +23,13 @@
 
 
 def turn_kernel(
-    samples, weights, table, turned, frames, filtered, coeffs, outbox, inbox, table_sem, send_sem, recv_sem
+    samples_hbm, weights_hbm, table, turned, samples, weights, frames, filtered, coeffs, outbox, inbox, sample_sem,
+    weight_sem, table_sem, send_sem, recv_sem, ring_sem
 ):
     position, core = lax.axis_index("inp"), lax.axis_index("tm")
-    group, layer = position // LAYERS, position % LAYERS
-    me = position * CORES + core
+    group, layer = position // LAYERS, lax.rem(position, LAYERS)
     groups, rows, length = coeffs.shape
-    devices = groups * LAYERS * CORES
-    inputs, _, _ = samples.shape
+    count, inputs, _ = samples.shape
     spectra = filtered.shape[0] // inputs
     taps = weights.shape[0]
     peers = LAYERS * CORES
@@ -44,32 +42,47 @@
         fetch(step).start()
         return carry
 
+    incoming = pltpu.make_async_copy(samples_hbm, samples, sample_sem)
+    incoming_weights = pltpu.make_async_copy(weights_hbm, weights, weight_sem)
+    incoming_weights.start()
+    incoming.start()
+
+    def greet_peers(sem):
+        for step in range(1, peers):
+            other = lax.rem(layer * CORES + core + step, peers)
+            pl.semaphore_signal(
+                sem, inc=1, device_id=(group * LAYERS + other // CORES, lax.rem(other, CORES)), device_id_type=MESH
+            )
+
+    def greet_groups(sem):
+        for step in range(1, groups):
+            other = lax.rem(group + step, groups)
+            pl.semaphore_signal(sem, inc=1, device_id=(other * LAYERS + layer, core), device_id_type=MESH)
+
+    barrier = pltpu.get_barrier_semaphore()
+    greet_peers(barrier)
+    greet_groups(barrier)
+
     lax.fori_loop(0, groups, start_fetch, 0)
 
-    barrier = pltpu.get_barrier_semaphore()
-
-    def greet(step, carry):
-        other = lax.rem(me + step, devices)
-        pl.semaphore_signal(
-            barrier, inc=1, device_id=(other // CORES, lax.rem(other, CORES)), device_id_type=MESH
-        )
-        return carry
-
-    lax.fori_loop(1, devices, greet, 0)
-
-    for a in range(inputs):
-        def columns(j, carry):
-            cols = pl.ds(pl.multiple_of(j * 128, 128), 128)
-            frames[...] = samples[a, :, cols].astype(jnp.float32)
-            total = weights[0:1, cols] * frames[0:spectra]
+    incoming_weights.wait()
+    incoming.wait()
+    def columns(j, carry):
+        cols = pl.ds(pl.multiple_of(j * 128, 128), 128)
+        for s in range(count):
+            frames[s // 2, s % 2 * inputs : (s % 2 + 1) * inputs, :] = samples[s, :, cols].astype(jnp.float32)
+        flat = frames.reshape(frames.shape[0] * 2 * inputs, 128)
+        for a in range(inputs):
+            total = weights[0:1, cols] * flat[pl.ds(a, spectra, stride=inputs), :]
             for tap in range(1, taps):
-                total = total + weights[tap : tap + 1, cols] * frames[tap : tap + spectra]
+                total = total + weights[tap : tap + 1, cols] * flat[pl.ds(a + tap * inputs, spectra, stride=inputs), :]
             filtered[a * spectra : (a + 1) * spectra, cols] = total.astype(jnp.bfloat16)
-            return carry
-
-        lax.fori_loop(0, length // 128, columns, 0)
-
-    pl.semaphore_wait(barrier, devices - 1)
+        return carry
+
+    lax.fori_loop(0, length // 128, columns, 0)
+
+    pl.semaphore_wait(barrier, peers + groups - 2)
+    greet_groups(ring_sem)
 
     half = filtered.shape[0] // 2
 
@@ -108,7 +121,9 @@
                     remote()
         return carry
 
-    lax.fori_loop(0, groups, send_group, 0)
+    send_group(0, 0)
+    pl.semaphore_wait(ring_sem, groups - 1)
+    lax.fori_loop(1, groups, send_group, 0)
 
     size = rows * 2
     out_row = lax.broadcasted_iota(jnp.int32, (size, size), 0)
@@ -139,38 +154,41 @@
         return carry
 
     lax.fori_loop(0, groups, receive_group, 0)
-    sent = outbox.at[pl.ds(0, devices - 1)]
+    sent = outbox.at[pl.ds(0, groups * peers - 1)]
     pltpu.make_async_copy(sent, sent, send_sem).wait()
 
 
-def gram_kernel(planes, out):
-    real, imag = planes[0], planes[1]
-    size = out.shape[1]
+def gram_kernel(planes, out, result, out_sem):
+    channels, size, _ = result.shape
     half = size // 2
+    row = lax.broadcasted_iota(jnp.int32, (half, half), 0)
+    column = lax.broadcasted_iota(jnp.int32, (half, half), 1)
+    lower = row >= column
 
     def times(a, b):
         return lax.dot_general(a, b, (((1,), (1,)), ((), ())), preferred_element_type=jnp.float32)
 
-    for i in range(2):
-        for j in range(2):
-            ri, rj = real[i * half : (i + 1) * half], real[j * half : (j + 1) * half]
-            mi, mj = imag[i * half : (i + 1) * half], imag[j * half : (j + 1) * half]
-            place = (0, slice(i * half, (i + 1) * half), slice(j * half, (j + 1) * half))
-            if i > j:
-                out[place] = times(ri, rj) + times(mi, mj)
-            elif i < j:
-                out[place] = times(mi, rj) - times(ri, mj)
-            else:
-                row = lax.broadcasted_iota(jnp.int32, (half, half), 0)
-                column = lax.broadcasted_iota(jnp.int32, (half, half), 1)
-                same = times(ri, rj) + times(mi, mj)
-                cross = times(mi, rj) - times(ri, mj)
-                out[place] = jnp.where(row >= column, same, cross)
+    def deliver(c):
+        return pltpu.make_async_copy(result.at[c], out.at[c], out_sem.at[c])
+
+    for c in range(channels):
+        real, imag = planes[2 * c], planes[2 * c + 1]
+        both = jnp.concatenate([real, imag], axis=1)
+        turned = jnp.concatenate([imag, -real], axis=1)
+        left = times(jnp.concatenate([both, turned[:half]], axis=0), both[:half])
+        right = times(jnp.concatenate([turned, both[half:]], axis=0), both[half:])
+        result[c, :half, :half] = jnp.where(lower, left[:half], left[size:])
+        result[c, half:, :half] = left[half:size]
+        result[c, :half, half:] = right[:half]
+        result[c, half:, half:] = jnp.where(lower, right[size:], right[half:size])
+        deliver(c).start()
+    for c in range(channels):
+        deliver(c).wait()
 
 
 def body(samples, pfb_weights):
-    frames = samples[:, 0]
-    inputs, count, length = frames.shape
+    frames = jnp.transpose(samples[:, 0], (1, 0, 2))
+    count, inputs, length = frames.shape
     taps = pfb_weights.shape[0]
     spectra = count - taps + 1
     channels = length // 2
@@ -188,32 +206,40 @@
         turn_kernel,
         out_shape=jax.ShapeDtypeStruct((per_device * 2, inputs * positions, all_spectra), jnp.bfloat16),
         in_specs=[
-            pl.BlockSpec(memory_space=pltpu.VMEM),
-            pl.BlockSpec(memory_space=pltpu.VMEM),
-            pl.BlockSpec(memory_space=pl.ANY),
+            pl.BlockSpec(memory_space=pltpu.HBM),
+            pl.BlockSpec(memory_space=pltpu.HBM),
+            pl.BlockSpec(memory_space=pltpu.HBM),
         ],
         out_specs=pl.BlockSpec(memory_space=pltpu.VMEM),
         scratch_shapes=[
-            pltpu.VMEM((count, 128), jnp.float32),
+            pltpu.VMEM((count, inputs, length), jnp.bfloat16),
+            pltpu.VMEM((taps, length), jnp.float32),
+            pltpu.VMEM(((count + 1) // 2, 2 * inputs, 128), jnp.float32),
             pltpu.VMEM((inputs * spectra, length), jnp.bfloat16),
             pltpu.VMEM((groups, rows, length), jnp.bfloat16),
             pltpu.VMEM((devices, deep, width), jnp.bfloat16),
             pltpu.VMEM((CORES, positions, deep, width), jnp.bfloat16),
+            pltpu.SemaphoreType.DMA,
+            pltpu.SemaphoreType.DMA,
             pltpu.SemaphoreType.DMA((groups,)),
             pltpu.SemaphoreType.DMA,
             pltpu.SemaphoreType.DMA((groups,)),
+            pltpu.SemaphoreType.REGULAR,
         ],
         compiler_params=pltpu.CompilerParams(
             collective_id=0, has_side_effects=True, vmem_limit_bytes=VMEM_LIMIT
         ),
-    )(frames, pfb_weights, table)
+    )(*(pltpu.with_memory_space_constraint(x, pltpu.HBM) for x in (frames, pfb_weights, table)))
     total = inputs * positions
     return pl.pallas_call(
         gram_kernel,
-        grid=(per_device,),
         out_shape=jax.ShapeDtypeStruct((per_device, total, total), jnp.float32),
-        in_specs=[pl.BlockSpec((2, total, all_spectra), lambda c: (c, 0, 0))],
-        out_specs=pl.BlockSpec((1, total, total), lambda c: (c, 0, 0)),
+        in_specs=[pl.BlockSpec(memory_space=pltpu.VMEM)],
+        out_specs=pl.BlockSpec(memory_space=pl.ANY),
+        scratch_shapes=[
+            pltpu.VMEM((per_device, total, total), jnp.float32),
+            pltpu.SemaphoreType.DMA((per_device,)),
+        ],
         compiler_params=pltpu.CompilerParams(vmem_limit_bytes=VMEM_LIMIT),
     )(turned)
 

time: 71.4 us -> 64.1 us (0.90)
  Pallas kernels: 68.5 us -> 64 us
  local copies, waits for them, and re-layouts: 2.79 us -> 0 us
    pallas_call x1, Pallas kernels: 64.7 us -> 61.2 us  [body(): pl.pallas_call(turn_kernel, out_shape=jax.ShapeDtypeStruct((per_device *...]
    unnamed x3 -> x0, local copies, waits for them, and re-layouts: 2.79 us -> none
    pallas_call x1, Pallas kernels: 3.8 us -> 2.84 us  [body(): pl.pallas_call(gram_kernel, out_shape=jax.ShapeDtypeStruct((per_device, t...]
where the time goes in v2:
time: 64.1 us; the launch traced here: 64 us
  Pallas kernels  64 us (100%)
    pallas_call x1, Pallas kernels, body(): pl.pallas_call(turn_kernel, out_shape=jax.ShapeDtypeStruct((per_device *...  61.2 us
    pallas_call x1, Pallas kernels, body(): pl.pallas_call(gram_kernel, out_shape=jax.ShapeDtypeStruct((per_device, t...  2.84 us

profile of v2, /device:TPU:1, one launch (start us, length us, event | category | flops | bytes accessed | tf_op | source)
XLA Modules:
  0.0 64.0 jit_solution(8468831591580971730)
XLA Ops:
  0.0 61.2 %shard_map.37.planes = bf16[8,512,256]{2,1,0:T(8,128)(2,1)S(1)} custom-call(bf16[131,4,2048]{2,1,0:T(4,128)(2,1)} %bitcast.3, f32[4,2048]{1,0:T(4,128)} %weights_hbm.1, bf16[16,128,2048]{2,1,0:T(8,128)(2,1)} %constant.2.clone.table), custom_call_target="tpu_custom_call" | custom-call | tf_op jit(solution)/shard_map/pallas_call | solution.py:205
  61.2 2.8 %shard_map.38 = f32[4,512,512]{2,1,0:T(8,128)} custom-call(bf16[8,512,256]{2,1,0:T(8,128)(2,1)S(1)} %shard_map.37.planes), custom_call_target="tpu_custom_call" | custom-call | tf_op jit(solution)/shard_map/pallas_call | solution.py:234

commit v3 on v2

--- a/solution.py
+++ b/solution.py
@@ -13,6 +13,7 @@
 VMEM_LIMIT = 48 * 1024 * 1024
 LAYERS = 8
 CORES = 2
+ORDER = (4, 5, 3, 6, 2, 7, 1, 0)
 
 
 def dft_table(channels, length, scale):
@@ -23,7 +24,7 @@
 
 
 def turn_kernel(
-    samples_hbm, weights_hbm, table, turned, samples, weights, frames, filtered, coeffs, outbox, inbox, sample_sem,
+    samples_hbm, weights_hbm, table, turned, samples, weights, frames, filtered, coeffs, outbox, inbox, first_sum, sample_sem,
     weight_sem, table_sem, send_sem, recv_sem, ring_sem
 ):
     position, core = lax.axis_index("inp"), lax.axis_index("tm")
@@ -42,10 +43,19 @@
         fetch(step).start()
         return carry
 
-    incoming = pltpu.make_async_copy(samples_hbm, samples, sample_sem)
+    pieces = sample_sem.shape[0]
+    piece = length // pieces
+    wide = 256
+
+    def incoming(k):
+        cols = pl.ds(k * piece, piece)
+        return pltpu.make_async_copy(samples_hbm.at[:, :, cols], samples.at[:, :, cols], sample_sem.at[k])
+
     incoming_weights = pltpu.make_async_copy(weights_hbm, weights, weight_sem)
     incoming_weights.start()
-    incoming.start()
+    for k in range(pieces):
+        incoming(k).start()
+    fetch(0).start()
 
     def greet_peers(sem):
         for step in range(1, peers):
@@ -54,75 +64,95 @@
                 sem, inc=1, device_id=(group * LAYERS + other // CORES, lax.rem(other, CORES)), device_id_type=MESH
             )
 
+    def greet_group(sem, step):
+        other = lax.rem(group + step, groups)
+        pl.semaphore_signal(sem, inc=1, device_id=(other * LAYERS + layer, core), device_id_type=MESH)
+
     def greet_groups(sem):
         for step in range(1, groups):
-            other = lax.rem(group + step, groups)
-            pl.semaphore_signal(sem, inc=1, device_id=(other * LAYERS + layer, core), device_id_type=MESH)
+            greet_group(sem, step)
 
     barrier = pltpu.get_barrier_semaphore()
+    greet_groups(barrier)
     greet_peers(barrier)
-    greet_groups(barrier)
-
-    lax.fori_loop(0, groups, start_fetch, 0)
+
+    def times(a, b):
+        return lax.dot_general(a, b, (((1,), (1,)), ((), ())), preferred_element_type=jnp.float32)
+
+    def combine(j):
+        for part in range(wide // 128):
+            cols = pl.ds(pl.multiple_of(j * wide + part * 128, 128), 128)
+            for s in range(count):
+                frames[part, s // 2, s % 2 * inputs : (s % 2 + 1) * inputs, :] = samples[s, :, cols].astype(jnp.float32)
+            flat = frames.at[part].reshape(frames.shape[1] * 2 * inputs, 128)
+            for a in range(inputs):
+                total = weights[0:1, cols] * flat[pl.ds(a, spectra, stride=inputs), :]
+                for tap in range(1, taps):
+                    total = total + weights[tap : tap + 1, cols] * flat[pl.ds(a + tap * inputs, spectra, stride=inputs), :]
+                filtered[a * spectra : (a + 1) * spectra, cols] = total.astype(jnp.bfloat16)
+
+    def partial(j):
+        cols = pl.ds(pl.multiple_of(j * wide, wide), wide)
+        return times(coeffs[0, :, cols], filtered[:, cols])
 
     incoming_weights.wait()
-    incoming.wait()
-    def columns(j, carry):
-        cols = pl.ds(pl.multiple_of(j * 128, 128), 128)
-        for s in range(count):
-            frames[s // 2, s % 2 * inputs : (s % 2 + 1) * inputs, :] = samples[s, :, cols].astype(jnp.float32)
-        flat = frames.reshape(frames.shape[0] * 2 * inputs, 128)
-        for a in range(inputs):
-            total = weights[0:1, cols] * flat[pl.ds(a, spectra, stride=inputs), :]
-            for tap in range(1, taps):
-                total = total + weights[tap : tap + 1, cols] * flat[pl.ds(a + tap * inputs, spectra, stride=inputs), :]
-            filtered[a * spectra : (a + 1) * spectra, cols] = total.astype(jnp.bfloat16)
-        return carry
-
-    lax.fori_loop(0, length // 128, columns, 0)
-
-    pl.semaphore_wait(barrier, peers + groups - 2)
-    greet_groups(ring_sem)
+    per_piece = piece // wide
+    last = length // wide
+    signals = 4
+    for j in range(last):
+        if j % per_piece == 0:
+            incoming(j // per_piece).wait()
+        if j == last // 2:
+            pl.semaphore_wait(barrier, peers + groups - 2)
+        if j >= last // 2:
+            first_step = 1 + (j - last // 2) * signals
+            for step in range(first_step, min(first_step + signals, groups)):
+                greet_group(ring_sem, step)
+        combine(j)
+        if j == 0:
+            fetch(0).wait()
+            first_sum[...] = partial(0)
+        else:
+            first_sum[...] += partial(j)
+    lax.fori_loop(1, groups, start_fetch, 0)
 
     half = filtered.shape[0] // 2
 
-    def send_group(step, carry):
-        fetch(step).wait()
-        found = lax.dot_general(
-            coeffs[step], filtered[...], (((1,), (1,)), ((), ())), preferred_element_type=jnp.float32
-        )
+    def make_group(step):
+        if isinstance(step, int):
+            found = first_sum[...]
+        else:
+            fetch(step).wait()
+            found = times(coeffs[step], filtered[...])
         found = found.reshape(peers, rows // peers, 2 * half)
         message = jnp.concatenate([found[:, :, :half], found[:, :, half:]], axis=1)
         outbox[pl.ds(step * peers, peers)] = message.astype(jnp.bfloat16)
-        to_group = lax.rem(group + step, groups)
-        for turn in (4, 3, 5, 2, 6, 1, 7, 0):
-            for flip in (0, 1):
-                to_layer = lax.rem(layer + turn, LAYERS)
-                to_core = lax.rem(core + flip, CORES)
-                source = outbox.at[step * peers + to_layer * CORES + to_core]
-
-                def remote():
-                    pltpu.make_async_remote_copy(
-                        src_ref=source,
-                        dst_ref=inbox.at[core, position],
-                        send_sem=send_sem,
-                        recv_sem=recv_sem.at[group],
-                        device_id=(to_group * LAYERS + to_layer, to_core),
-                        device_id_type=MESH,
-                    ).start()
-
-                if turn == 0 and flip == 0:
-                    pl.when(step > 0)(remote)
-
-                    @pl.when(step == 0)
-                    def _():
-                        pltpu.make_async_copy(source, inbox.at[core, position], recv_sem.at[group]).start()
-                else:
-                    remote()
+
+    def send(step, to_layer, to_core):
+        pltpu.make_async_remote_copy(
+            src_ref=outbox.at[step * peers + to_layer * CORES + to_core],
+            dst_ref=inbox.at[core, position],
+            send_sem=send_sem,
+            recv_sem=recv_sem.at[group],
+            device_id=(lax.rem(group + step, groups) * LAYERS + to_layer, to_core),
+            device_id_type=MESH,
+        ).start()
+
+    make_group(0)
+    for turn in ORDER:
+        for flip in (0, 1):
+            if turn or flip:
+                send(0, lax.rem(layer + turn, LAYERS), lax.rem(core + flip, CORES))
+    pltpu.make_async_copy(outbox.at[layer * CORES + core], inbox.at[core, position], recv_sem.at[group]).start()
+    pl.semaphore_wait(ring_sem, groups - 1)
+
+    def send_group(step, carry):
+        make_group(step)
+        for turn in ORDER:
+            for flip in range(CORES):
+                send(step, lax.rem(layer + turn, LAYERS), lax.rem(core + flip, CORES))
         return carry
 
-    send_group(0, 0)
-    pl.semaphore_wait(ring_sem, groups - 1)
     lax.fori_loop(1, groups, send_group, 0)
 
     size = rows * 2
@@ -214,12 +244,13 @@
         scratch_shapes=[
             pltpu.VMEM((count, inputs, length), jnp.bfloat16),
             pltpu.VMEM((taps, length), jnp.float32),
-            pltpu.VMEM(((count + 1) // 2, 2 * inputs, 128), jnp.float32),
+            pltpu.VMEM((2, (count + 1) // 2, 2 * inputs, 128), jnp.float32),
             pltpu.VMEM((inputs * spectra, length), jnp.bfloat16),
             pltpu.VMEM((groups, rows, length), jnp.bfloat16),
             pltpu.VMEM((devices, deep, width), jnp.bfloat16),
             pltpu.VMEM((CORES, positions, deep, width), jnp.bfloat16),
-            pltpu.SemaphoreType.DMA,
+            pltpu.VMEM((rows, inputs * spectra), jnp.float32),
+            pltpu.SemaphoreType.DMA((4,)),
             pltpu.SemaphoreType.DMA,
             pltpu.SemaphoreType.DMA((groups,)),
             pltpu.SemaphoreType.DMA,

time: 64.1 us -> 63.5 us (level)
  no operation moved by 1% of the time
where the time goes in v3:
time: 63.5 us; the launch traced here: 63.4 us
  Pallas kernels  63.4 us (100%)
    pallas_call x1, Pallas kernels, body(): pl.pallas_call(turn_kernel, out_shape=jax.ShapeDtypeStruct((per_device *...  60.6 us
    pallas_call x1, Pallas kernels, body(): pl.pallas_call(gram_kernel, out_shape=jax.ShapeDtypeStruct((per_device, t...  2.84 us

profile of v3, /device:TPU:1, one launch (start us, length us, event | category | flops | bytes accessed | tf_op | source)
XLA Modules:
  0.0 63.4 jit_solution(6559573266136519059)
XLA Ops:
  0.0 60.6 %shard_map.37.planes = bf16[8,512,256]{2,1,0:T(8,128)(2,1)S(1)} custom-call(bf16[131,4,2048]{2,1,0:T(4,128)(2,1)} %bitcast.3, f32[4,2048]{1,0:T(4,128)} %weights_hbm.1, bf16[16,128,2048]{2,1,0:T(8,128)(2,1)} %constant.2.clone.table), custom_call_target="tpu_custom_call" | custom-call | tf_op jit(solution)/shard_map/pallas_call | solution.py:235
  60.6 2.8 %shard_map.38 = f32[4,512,512]{2,1,0:T(8,128)} custom-call(bf16[8,512,256]{2,1,0:T(8,128)(2,1)S(1)} %shard_map.37.planes), custom_call_target="tpu_custom_call" | custom-call | tf_op jit(solution)/shard_map/pallas_call | solution.py:265

commit v4 on v3

v4 whole, which is shorter than its diff:
```python
import functools
import math
import jax
import jax.numpy as jnp
import ml_dtypes
import numpy as np
from jax import lax
from jax.experimental import pallas as pl
from jax.experimental.pallas import tpu as pltpu
from jax.sharding import PartitionSpec as P

MESH = pl.DeviceIdType.MESH
VMEM_LIMIT = 48 * 1024 * 1024
LAYERS = 8
CORES = 2
PASSES = 2
ORDER = (4, 5, 3, 6, 2, 7, 1, 0)


def dft_table(channels, length, scale):
    phase = np.arange(channels)[:, None] * np.arange(length)[None, :] % length
    angle = np.arange(length) * (2.0 * math.pi / length)
    rows = np.stack([np.cos(angle)[phase], -np.sin(angle)[phase]], axis=1) * scale
    return rows.reshape(channels * 2, length).astype(ml_dtypes.bfloat16)


def turn_kernel(
    samples_hbm, weights_hbm, table, done, late, early, samples, weights, frames, filtered, coeffs, outbox, inbox, first_sum, sample_sem,
    weight_sem, table_sem, send_sem, recv_sem, ring_sem
):
    position, core = lax.axis_index("inp"), lax.axis_index("tm")
    group, layer = position // LAYERS, lax.rem(position, LAYERS)
    groups, rows, length = coeffs.shape
    count, inputs, _ = samples.shape
    spectra = filtered.shape[0] // inputs
    taps = weights.shape[0]
    peers = LAYERS * CORES

    def fetch(step):
        chunk = lax.rem(group + step, groups)
        return pltpu.make_async_copy(table.at[chunk], coeffs.at[step], table_sem.at[step])

    def start_fetch(step, carry):
        fetch(step).start()
        return carry

    pieces = sample_sem.shape[0]
    piece = length // pieces
    wide = 256

    def incoming(k):
        cols = pl.ds(k * piece, piece)
        return pltpu.make_async_copy(samples_hbm.at[:, :, cols], samples.at[:, :, cols], sample_sem.at[k])

    incoming_weights = pltpu.make_async_copy(weights_hbm, weights, weight_sem)
    incoming_weights.start()
    for k in range(pieces):
        incoming(k).start()
    fetch(0).start()

    def greet_peers(sem):
        for step in range(1, peers):
            other = lax.rem(layer * CORES + core + step, peers)
            pl.semaphore_signal(
                sem, inc=1, device_id=(group * LAYERS + other // CORES, lax.rem(other, CORES)), device_id_type=MESH
            )

    def greet_group(sem, step):
        other = lax.rem(group + step, groups)
        pl.semaphore_signal(sem, inc=1, device_id=(other * LAYERS + layer, core), device_id_type=MESH)

    def greet_groups(sem):
        for step in range(1, groups):
            greet_group(sem, step)

    barrier = pltpu.get_barrier_semaphore()
    greet_groups(barrier)
    greet_peers(barrier)

    def times(a, b):
        return lax.dot_general(a, b, (((1,), (1,)), ((), ())), preferred_element_type=jnp.float32)

    def combine(j):
        for part in range(wide // 128):
            cols = pl.ds(pl.multiple_of(j * wide + part * 128, 128), 128)
            for s in range(count):
                frames[part, s // 2, s % 2 * inputs : (s % 2 + 1) * inputs, :] = samples[s, :, cols].astype(jnp.float32)
            flat = frames.at[part].reshape(frames.shape[1] * 2 * inputs, 128)
            for a in range(inputs):
                total = weights[0:1, cols] * flat[pl.ds(a, spectra, stride=inputs), :]
                for tap in range(1, taps):
                    total = total + weights[tap : tap + 1, cols] * flat[pl.ds(a + tap * inputs, spectra, stride=inputs), :]
                filtered[a * spectra : (a + 1) * spectra, cols] = total.astype(jnp.bfloat16)

    def partial(j):
        cols = pl.ds(pl.multiple_of(j * wide, wide), wide)
        return times(coeffs[0, :, cols], filtered[:, cols])

    incoming_weights.wait()
    per_piece = piece // wide
    last = length // wide
    signals = 4
    for j in range(last):
        if j % per_piece == 0:
            incoming(j // per_piece).wait()
        if j == last // 2:
            pl.semaphore_wait(barrier, peers + groups - 2)
        if j >= last // 2:
            first_step = 1 + (j - last // 2) * signals
            for step in range(first_step, min(first_step + signals, groups)):
                greet_group(ring_sem, step)
        combine(j)
        if j == 0:
            fetch(0).wait()
            first_sum[...] = partial(0)
        else:
            first_sum[...] += partial(j)
    lax.fori_loop(1, groups, start_fetch, 0)

    per_pass = groups * peers
    deep = outbox.shape[1]

    def make_group(step):
        if isinstance(step, int):
            found = first_sum[...]
        else:
            fetch(step).wait()
            found = times(coeffs[step], filtered[...])
        found = found.reshape(peers, rows // peers, inputs * spectra)
        size = rows // peers // PASSES
        front = lax.broadcasted_iota(jnp.int32, (peers, rows // peers, spectra), 1) < size
        pairs = [[], []]
        for a in range(0, inputs, 2):
            one = found[:, :, a * spectra : (a + 1) * spectra]
            two = found[:, :, (a + 1) * spectra : (a + 2) * spectra]
            pairs[0].append(jnp.where(front, one, pltpu.roll(two, size, 1)))
            pairs[1].append(jnp.where(front, pltpu.roll(one, size, 1), two))
        for turn in range(PASSES):
            message = jnp.concatenate(pairs[turn], axis=1).astype(jnp.bfloat16)
            outbox[pl.ds(turn * per_pass + step * peers, peers)] = message

    def send(turn, step, to_layer, to_core):
        pltpu.make_async_remote_copy(
            src_ref=outbox.at[turn * per_pass + step * peers + to_layer * CORES + to_core],
            dst_ref=inbox.at[turn, core, position],
            send_sem=send_sem,
            recv_sem=recv_sem.at[turn, group],
            device_id=(lax.rem(group + step, groups) * LAYERS + to_layer, to_core),
            device_id_type=MESH,
        ).start()

    def send_ring(turn, step):
        for away in ORDER:
            for flip in range(CORES):
                send(turn, step, lax.rem(layer + away, LAYERS), lax.rem(core + flip, CORES))

    def send_own_ring(turn):
        for away in ORDER:
            for flip in range(CORES):
                if away or flip:
                    send(turn, 0, lax.rem(layer + away, LAYERS), lax.rem(core + flip, CORES))
        own = outbox.at[turn * per_pass + layer * CORES + core]
        pltpu.make_async_copy(own, inbox.at[turn, core, position], recv_sem.at[turn, group]).start()

    make_group(0)
    send_own_ring(0)
    pl.semaphore_wait(ring_sem, groups - 1)

    def first_pass(step, carry):
        make_group(step)
        send_ring(0, step)
        return carry

    def second_pass(step, carry):
        send_ring(1, step)
        return carry

    lax.fori_loop(1, groups, first_pass, 0)
    send_own_ring(1)
    lax.fori_loop(1, groups, second_pass, 0)

    size = LAYERS * deep
    strip = LAYERS * inputs
    planes = size // strip
    out_row = lax.broadcasted_iota(jnp.int32, (size, size), 0)
    in_row = lax.broadcasted_iota(jnp.int32, (size, size), 1)
    permute = jnp.where(in_row == out_row % strip * planes + out_row // strip, 1.0, 0.0).astype(jnp.bfloat16)

    def receive(turn, ordered_planes):
        def receive_group(step, carry):
            from_group = lax.rem(group + groups - step, groups)
            place = pl.ds(from_group * LAYERS, LAYERS)
            landed = inbox.at[turn, :, place]
            pltpu.make_async_copy(landed, landed, recv_sem.at[turn, from_group]).wait()
            both = jnp.concatenate([inbox[turn, t, place].reshape(size, spectra) for t in range(CORES)], axis=1)
            ordered = jnp.dot(permute, both, preferred_element_type=jnp.float32).astype(jnp.bfloat16)
            where = pl.ds(pl.multiple_of(from_group * strip, strip), strip)
            for plane in range(planes):
                ordered_planes[plane, where, :] = ordered[plane * strip : (plane + 1) * strip]
            return carry

        lax.fori_loop(0, groups, receive_group, 0)

    receive(0, early)
    for c in range(done.shape[0]):
        visibilities(early[2 * c], early[2 * c + 1], done, c)
    receive(1, late)
    sent = outbox.at[pl.ds(0, PASSES * (per_pass - 1))]
    pltpu.make_async_copy(sent, sent, send_sem).wait()


def visibilities(real, imag, result, c):
    size = real.shape[0]
    half = size // 2
    row = lax.broadcasted_iota(jnp.int32, (half, half), 0)
    column = lax.broadcasted_iota(jnp.int32, (half, half), 1)
    lower = row >= column

    def times(a, b):
        return lax.dot_general(a, b, (((1,), (1,)), ((), ())), preferred_element_type=jnp.float32)

    both = jnp.concatenate([real, imag], axis=1)
    turned = jnp.concatenate([imag, -real], axis=1)
    left = times(jnp.concatenate([both, turned[:half]], axis=0), both[:half])
    right = times(jnp.concatenate([turned, both[half:]], axis=0), both[half:])
    result[c, :half, :half] = jnp.where(lower, left[:half], left[size:])
    result[c, half:, :half] = left[half:size]
    result[c, :half, half:] = right[:half]
    result[c, half:, half:] = jnp.where(lower, right[size:], right[half:size])


def finish_kernel(done, planes, out, result, out_sem):
    first = done.shape[0]
    copies = [pltpu.make_async_copy(done.at[c], out.at[c], out_sem.at[c]) for c in range(first)]
    for copy in copies:
        copy.start()
    for c in range(result.shape[0]):
        visibilities(planes[2 * c], planes[2 * c + 1], result, c)
        copies.append(pltpu.make_async_copy(result.at[c], out.at[first + c], out_sem.at[first + c]))
        copies[-1].start()
    for copy in copies:
        copy.wait()


def body(samples, pfb_weights):
    frames = jnp.transpose(samples[:, 0], (1, 0, 2))
    count, inputs, length = frames.shape
    taps = pfb_weights.shape[0]
    spectra = count - taps + 1
    channels = length // 2
    positions = lax.axis_size("inp")
    groups = positions // LAYERS
    devices = positions * CORES
    rows = 2 * channels // groups
    all_spectra = spectra * CORES
    scale = math.sqrt(2.0 / length) / math.sqrt(all_spectra)
    table = jnp.asarray(dft_table(channels, length, scale).reshape(groups, rows, length))
    per_device = channels // devices
    total = inputs * positions
    share = per_device // PASSES
    deep = inputs * share * 2
    done, late = pl.pallas_call(
        turn_kernel,
        out_shape=[
            jax.ShapeDtypeStruct((share, total, total), jnp.float32),
            jax.ShapeDtypeStruct((share * 2, total, all_spectra), jnp.bfloat16),
        ],
        in_specs=[pl.BlockSpec(memory_space=pltpu.HBM)] * 3,
        out_specs=[pl.BlockSpec(memory_space=pltpu.VMEM)] * 2,
        scratch_shapes=[
            pltpu.VMEM((share * 2, total, all_spectra), jnp.bfloat16),
            pltpu.VMEM((count, inputs, length), jnp.bfloat16),
            pltpu.VMEM((taps, length), jnp.float32),
            pltpu.VMEM((2, (count + 1) // 2, 2 * inputs, 128), jnp.float32),
            pltpu.VMEM((inputs * spectra, length), jnp.bfloat16),
            pltpu.VMEM((groups, rows, length), jnp.bfloat16),
            pltpu.VMEM((PASSES * devices, deep, spectra), jnp.bfloat16),
            pltpu.VMEM((PASSES, CORES, positions, deep, spectra), jnp.bfloat16),
            pltpu.VMEM((rows, inputs * spectra), jnp.float32),
            pltpu.SemaphoreType.DMA((4,)),
            pltpu.SemaphoreType.DMA,
            pltpu.SemaphoreType.DMA((groups,)),
            pltpu.SemaphoreType.DMA,
            pltpu.SemaphoreType.DMA((PASSES, groups)),
            pltpu.SemaphoreType.REGULAR,
        ],
        compiler_params=pltpu.CompilerParams(
            collective_id=0, has_side_effects=True, vmem_limit_bytes=VMEM_LIMIT
        ),
    )(*(pltpu.with_memory_space_constraint(x, pltpu.HBM) for x in (frames, pfb_weights, table)))
    return pl.pallas_call(
        finish_kernel,
        out_shape=jax.ShapeDtypeStruct((per_device, total, total), jnp.float32),
        in_specs=[pl.BlockSpec(memory_space=pltpu.VMEM)] * 2,
        out_specs=pl.BlockSpec(memory_space=pl.ANY),
        scratch_shapes=[
            pltpu.VMEM((share, total, total), jnp.float32),
            pltpu.SemaphoreType.DMA((per_device,)),
        ],
        compiler_params=pltpu.CompilerParams(vmem_limit_bytes=VMEM_LIMIT),
    )(done, late)


def solution(mesh):
    placed = (P("inp", "tm", None, None), P())
    return jax.shard_map(
        body, mesh=mesh, in_specs=placed, out_specs=P(("inp", "tm"), None, None), check_vma=False
    )
```

time: 63.5 us -> 64.4 us (1.014)
  Pallas kernels: 63.4 us -> 64.3 us
    pallas_call x2, Pallas kernels: 63.4 us -> 64.3 us  [the longest x1 62.2 us: body(): pl.pallas_call(turn_kernel, out_shape=[jax.ShapeDtypeStruct((share, total...]
where the time goes in v4:
time: 64.4 us; the launch traced here: 64.3 us
  Pallas kernels  64.3 us (100%)
    pallas_call x1, Pallas kernels, body(): pl.pallas_call(turn_kernel, out_shape=[jax.ShapeDtypeStruct((share, total...  62.2 us
    pallas_call x1, Pallas kernels, body(): pl.pallas_call(finish_kernel, out_shape=jax.ShapeDtypeStruct((per_device,...  2.04 us

profile of v4, /device:TPU:1, one launch (start us, length us, event | category | flops | bytes accessed | tf_op | source)
XLA Modules:
  0.0 64.3 jit_solution(6234660105243814330)
XLA Ops:
  0.0 62.2 %shard_map.37 = (f32[2,512,512]{2,1,0:T(8,128)S(1)}, bf16[4,512,256]{2,1,0:T(8,128)(2,1)S(1)}) custom-call(bf16[131,4,2048]{2,1,0:T(4,128)(2,1)} %bitcast.3, f32[4,2048]{1,0:T(4,128)} %weights_hbm.1, bf16[16,128,2048]{2,1,0:T(8,128)(2,1)} %constant.2.clone.table), custom_call_target="tpu_custom_call" | custom-call | tf_op jit(solution)/shard_map/pallas_call | solution.py:262
  62.2 2.0 %shard_map.38 = f32[4,512,512]{2,1,0:T(8,128)} custom-call(f32[2,512,512]{2,1,0:T(8,128)S(1)} %get-tuple-element.7.done, bf16[4,512,256]{2,1,0:T(8,128)(2,1)S(1)} %get-tuple-element.8.planes), custom_call_target="tpu_custom_call" | custom-call | tf_op jit(solution)/shard_map/pallas_call | solution.py:291

commit v5 on v3

--- a/solution.py
+++ b/solution.py
@@ -144,10 +144,14 @@
             if turn or flip:
                 send(0, lax.rem(layer + turn, LAYERS), lax.rem(core + flip, CORES))
     pltpu.make_async_copy(outbox.at[layer * CORES + core], inbox.at[core, position], recv_sem.at[group]).start()
-    pl.semaphore_wait(ring_sem, groups - 1)
 
     def send_group(step, carry):
         make_group(step)
+
+        @pl.when(step == 1)
+        def _():
+            pl.semaphore_wait(ring_sem, groups - 1)
+
         for turn in ORDER:
             for flip in range(CORES):
                 send(step, lax.rem(layer + turn, LAYERS), lax.rem(core + flip, CORES))

time: 63.5 us -> 63.5 us (level)
  no operation moved by 1% of the time
where the time goes in v5:
time: 63.5 us; the launch traced here: 63.4 us
  Pallas kernels  63.4 us (100%)
    pallas_call x1, Pallas kernels, body(): pl.pallas_call(turn_kernel, out_shape=jax.ShapeDtypeStruct((per_device *...  60.5 us
    pallas_call x1, Pallas kernels, body(): pl.pallas_call(gram_kernel, out_shape=jax.ShapeDtypeStruct((per_device, t...  2.84 us

profile of v5, /device:TPU:1, one launch (start us, length us, event | category | flops | bytes accessed | tf_op | source)
XLA Modules:
  0.0 63.4 jit_solution(5625253224711919467)
XLA Ops:
  0.0 60.5 %shard_map.37.planes = bf16[8,512,256]{2,1,0:T(8,128)(2,1)S(1)} custom-call(bf16[131,4,2048]{2,1,0:T(4,128)(2,1)} %bitcast.3, f32[4,2048]{1,0:T(4,128)} %weights_hbm.1, bf16[16,128,2048]{2,1,0:T(8,128)(2,1)} %constant.2.clone.table), custom_call_target="tpu_custom_call" | custom-call | tf_op jit(solution)/shard_map/pallas_call | solution.py:239
  60.5 2.8 %shard_map.38 = f32[4,512,512]{2,1,0:T(8,128)} custom-call(bf16[8,512,256]{2,1,0:T(8,128)(2,1)S(1)} %shard_map.37.planes), custom_call_target="tpu_custom_call" | custom-call | tf_op jit(solution)/shard_map/pallas_call | solution.py:269
